TPU v7x, 512 devices: a whole 4x4x16 slice. The times are simulated.
512 devices in a mesh: ht: 16 (over z_lo, core), wt: 32 (over x, y, z_hi).
Axes of the slice: x: 4, y: 4, z: 16 (z_hi: 2, z_lo: 8; z = z_hi * 8 + z_lo), core: 2. Of those that a mesh axis runs over, the one named last changes fastest.
Arguments:
- queries: bfloat16 [256, 256, 1024], P('ht', 'wt'), may hold values from -30 to 30
- keys_new: bfloat16 [256, 256, 1024], P('ht', 'wt'), may hold values from -10 to 10, as said below
- values_new: bfloat16 [256, 256, 1024], P('ht', 'wt'), may hold values from -6 to 6
- keys_cache: bfloat16 [1, 256, 256, 1024], P(None, 'ht', 'wt'), may hold values from -10 to 10, as said below
- values_cache: bfloat16 [1, 256, 256, 1024], P(None, 'ht', 'wt'), may hold values from -6 to 6
- conv_weight: float32 [3, 3, 1024], replicated, may hold values from -2 to 2
- conv_bias: float32 [1024], replicated, may hold values from -2.5 to 2.5
Outputs:
- block_out: bfloat16 [256, 256, 1024], P('ht', 'wt')
Inputs may be any that keep to these rules, and one draw needn't show every extreme that they name: `keys_new`: key features. `keys_cache`: key features.
All inputs are finite; a program needn't handle non-finite values.
Results may differ from a plain program's by a relative error of at most 0.003.
Values may be sent and summed in bfloat16 or wider, within the bound.
A program may use at most 64 MiB of HBM per device.

v0:
```python
import jax
import jax.numpy as jnp
from jax import lax
from jax.sharding import PartitionSpec as P

HD = 128
WIN = 32


def with_halo(block, sides, width):
    for axis, dim in sides:
        count = lax.axis_size(axis)
        forward = [(i, i + 1) for i in range(count - 1)]
        backward = [(target, source) for source, target in forward]
        low = lax.ppermute(
            lax.slice_in_dim(block, block.shape[dim] - width, None, axis=dim), axis, forward
        )
        high = lax.ppermute(lax.slice_in_dim(block, 0, width, axis=dim), axis, backward)
        block = jnp.concatenate([low, block, high], axis=dim)
    return block


def passed_along(value, axis, by):
    size = lax.axis_size(axis)
    pairs = [(i, i + by) for i in range(size) if 0 <= i + by < size]
    return lax.ppermute(value, axis, pairs)


def window_allowed(row_start, col_start, frame_rows, frame_cols, tile_rows, tile_cols, half_win):
    ext_rows = jnp.arange(tile_rows + 2 * half_win, dtype=jnp.int32) - half_win
    ext_cols = jnp.arange(tile_cols + 2 * half_win, dtype=jnp.int32) - half_win
    query_rows = jnp.arange(tile_rows, dtype=jnp.int32)
    query_cols = jnp.arange(tile_cols, dtype=jnp.int32)
    row_delta = ext_rows[None, :] - query_rows[:, None]
    col_delta = ext_cols[None, :] - query_cols[:, None]
    global_rows = row_start + ext_rows
    global_cols = col_start + ext_cols
    row_valid = (
        (row_delta >= -half_win)
        & (row_delta < half_win)
        & ((global_rows >= 0) & (global_rows < frame_rows))[None, :]
    )
    col_valid = (
        (col_delta >= -half_win)
        & (col_delta < half_win)
        & ((global_cols >= 0) & (global_cols < frame_cols))[None, :]
    )
    allowed = row_valid[:, None, :, None] & col_valid[None, :, None, :]
    return allowed.reshape(
        tile_rows * tile_cols, (tile_rows + 2 * half_win) * (tile_cols + 2 * half_win)
    )


def attend(query_rows, keys_flat, values_flat, allowed, heads, head_dim):
    score_scale = head_dim ** (-0.5)

    def one_head(head_index):
        lane_start = head_index * head_dim
        query_head = lax.dynamic_slice_in_dim(query_rows, lane_start, head_dim, 1)
        key_head = lax.dynamic_slice_in_dim(keys_flat, lane_start, head_dim, 1)
        value_head = lax.dynamic_slice_in_dim(values_flat, lane_start, head_dim, 1)
        scores = (
            jnp.einsum("qd,kd->qk", query_head, key_head, preferred_element_type=jnp.float32)
            * score_scale
        )
        scores = jnp.where(allowed, scores, -1e30)
        row_top = jnp.max(scores, axis=1, keepdims=True)
        weights_f = jnp.exp(scores - row_top)
        denominator = jnp.sum(weights_f, axis=1, keepdims=True)
        numerator = jnp.dot(
            weights_f.astype(jnp.bfloat16), value_head, preferred_element_type=jnp.float32
        )
        return numerator / denominator

    outputs = lax.map(one_head, jnp.arange(heads, dtype=jnp.int32))
    return outputs.transpose(1, 0, 2).reshape(query_rows.shape[0], heads * head_dim)


def local_conv(padded, conv_weight, conv_bias, tile_rows, tile_cols):
    enhanced = jnp.zeros((tile_rows, tile_cols, padded.shape[2]), jnp.float32) + conv_bias
    for row_shift in range(3):
        for col_shift in range(3):
            enhanced = (
                enhanced
                + padded[
                    row_shift : row_shift + tile_rows, col_shift : col_shift + tile_cols
                ].astype(jnp.float32)
                * conv_weight[row_shift, col_shift]
            )
    return enhanced


def cycle_conv(values_new, conv_weight, conv_bias):
    tile_rows, tile_cols, channels = values_new.shape
    padded = with_halo(values_new, (("ht", 0), ("wt", 1)), 1)
    return local_conv(padded, conv_weight, conv_bias, tile_rows, tile_cols)


def shards(queries, keys_new, values_new, keys_cache, values_cache, conv_weight, conv_bias):
    tile_rows, tile_cols, channels = queries.shape
    frames = keys_cache.shape[0] + 1
    half_win = WIN // 2
    stacked = jnp.concatenate([keys_cache, keys_new[None], values_cache, values_new[None]], axis=0)
    row_start = lax.axis_index("ht") * tile_rows
    frame_rows = tile_rows * lax.axis_size("ht")
    frame_cols = tile_cols * lax.axis_size("wt")
    tile_reach = (half_win + tile_cols - 1) // tile_cols
    distances = [span for span in range(tile_reach, 0, -1)] + [
        -span for span in range(1, tile_reach + 1)
    ]
    col_width = tile_cols + 2 * half_win
    taller = with_halo(stacked, (("ht", 1),), half_win)
    shifted = [passed_along(taller, "wt", distance) for distance in distances]
    joined = jnp.concatenate(shifted[:tile_reach] + [taller] + shifted[tile_reach:], axis=2)
    region_rows = tile_rows + 2 * half_win
    keys_flat = joined[:frames].reshape(frames * region_rows * col_width, channels)
    values_flat = joined[frames:].reshape(frames * region_rows * col_width, channels)
    col_start = lax.axis_index("wt") * tile_cols
    allowed = window_allowed(
        row_start, col_start, frame_rows, frame_cols, tile_rows, tile_cols, half_win
    )
    allowed = jnp.tile(allowed, (1, frames))
    attended = attend(
        queries.reshape(tile_rows * tile_cols, channels),
        keys_flat,
        values_flat,
        allowed,
        channels // HD,
        HD,
    )
    enhanced = cycle_conv(values_new, conv_weight, conv_bias)
    return (attended.reshape(tile_rows, tile_cols, channels) + enhanced).astype(jnp.bfloat16)


def solution(mesh):
    placed = (
        P("ht", "wt", None),
        P("ht", "wt", None),
        P("ht", "wt", None),
        P(None, "ht", "wt", None),
        P(None, "ht", "wt", None),
        P(),
        P(),
    )
    return jax.shard_map(
        shards, mesh=mesh, in_specs=placed, out_specs=P("ht", "wt", None), check_vma=False
    )
```

profile of v0, /device:TPU:47, one launch (start us, length us, event | category | flops | bytes accessed | tf_op | source)
XLA Modules:
  0.0 661.8 jit_solution(13551340014827714334)
XLA Ops:
  1.3 4.2 collective-permute-start
  5.6 1.9 collective-permute-start.1
  7.5 9.8 %collective-permute-done = bf16[4,16,8,1024]{3,2,1,0:T(8,128)(2,1)S(1)} collective-permute-done((bf16[4,16,8,1024]{3,2,1,0:T(8,128)(2,1)S(1)}, bf16[4,16,8,1024]{3,2,1,0:T(8,128)(2,1)S(1)}, u32[]{:S(2)}, u32[]{:S(2)}) %collective-permute-start) | collective-permute-done | bytes 1048608 | tf_op jit(solution)/shard_map/ppermute | solution.py:15
  17.3 4.4 collective-permute-done.1
  21.7 3.4 pad_maximum_fusion.1
  25.1 3.2 collective-permute-start.2
  28.3 13.6 %collective-permute-start.3 = (bf16[4,48,8,1024]{3,2,1,0:T(8,128)(2,1)}, bf16[4,48,8,1024]{3,2,1,0:T(8,128)(2,1)}, u32[]{:S(2)}, u32[]{:S(2)}) collective-permute-start(bf16[4,48,8,1024]{3,2,1,0:T(8,128)(2,1)} %pad_maximum_fusion.1), channel_id=1, source_target_pairs={{0,1},{1,2},{2,3},{3,4},{4,5},{5,6},{6,7},{7,8},{8,9},{9,10},{10,1... | collective-permute-start | bytes 9437192 | tf_op jit(solution)/shard_map/ppermute | solution.py:26
  42.0 1.9 collective-permute-start.4
  43.9 4.1 collective-permute-start.5
  48.0 2.6 collective-permute-start.6
  51.2 2.7 and.85
  55.2 520.1 %collective-permute-start.7 = (bf16[1,8,1024]{2,1,0:T(8,128)(2,1)S(1)}, bf16[1,8,1024]{2,1,0:T(8,128)(2,1)S(1)}, u32[]{:S(2)}, u32[]{:S(2)}) collective-permute-start(bf16[1,8,1024]{2,1,0:T(8,128)(2,1)S(1)} %get-tuple-element.87), channel_id=1, source_target_pairs={{32,0},{64,32},{96,64},{128,96},{160,128},{192,160},{224,192},{256... | collective-permute-start | bytes 49160 | tf_op jit(solution)/shard_map/ppermute | solution.py:18
  575.4 7.3 %collective-permute-done.7 = bf16[1,8,1024]{2,1,0:T(8,128)(2,1)S(1)} collective-permute-done((bf16[1,8,1024]{2,1,0:T(8,128)(2,1)S(1)}, bf16[1,8,1024]{2,1,0:T(8,128)(2,1)S(1)}, u32[]{:S(2)}, u32[]{:S(2)}) %collective-permute-start.7) | collective-permute-done | bytes 16416 | tf_op jit(solution)/shard_map/ppermute | solution.py:18
  582.9 1.9 collective-permute-start.8
  584.8 13.0 %collective-permute-start.9 = (bf16[18,1,1024]{2,1,0:T(2,128)(2,1)S(1)}, bf16[18,1,1024]{2,1,0:T(2,128)(2,1)S(1)}, u32[]{:S(2)}, u32[]{:S(2)}) collective-permute-start(bf16[18,1,1024]{2,1,0:T(2,128)(2,1)S(1)} %get-tuple-element.86), channel_id=1, source_target_pairs={{1,0},{2,1},{3,2},{4,3},{5,4},{6,5},{7,6},{8,7},{9,8},{10,9},{11,1... | collective-permute-start | bytes 110600 | tf_op jit(solution)/shard_map/ppermute | solution.py:18
  597.8 2.2 constant_dynamic-update-slice_fusion.3
  600.1 2.3 constant_dynamic-update-slice_fusion.2
  602.9 2.2 constant_dynamic-update-slice_fusion.1
  605.1 2.2 constant_dynamic-update-slice_fusion
  607.4 6.0 fusion.28
  613.4 46.5 %while.11 = (s32[]{:T(128)}, f32[8,128,128]{2,1,0:T(8,128)S(1)}, s32[8]{0:T(128)S(1)}, bf16[128,1024]{1,0:T(8,128)(2,1)}, bf16[3840,1024]{1,0:T(8,128)(2,1)}, /*...) while((s32[]{:T(128)}, f32[8,128,128]{2,1,0:T(8,128)S(1)}, ...), condition=%wide.region_3.4_spmd.clone, body=%wide.region_0.3_spmd.clone.sunk | while | flops 255115008 | bytes 10178731 | solution.py:75
  621.0 1.8 fusion.39
  632.6 1.8 fusion.39
  655.9 1.8 fusion.39
  (85 shorter events, 41.9 us)
Async XLA Ops:
  1.3 46.7 %copy-start = (bf16[16,8,1024]{2,1,0:T(8,128)(2,1)S(1)}, bf16[16,8,1024]{2,1,0:T(8,128)(2,1)}, u32[]{:S(2)}) copy-start(bf16[16,8,1024]{2,1,0:T(8,128)(2,1)} %param.11) | copy-start | bytes 786436
  1.3 49.8 %copy-start.4 = (f32[3,3,1024]{2,1,0:T(4,128)S(1)}, f32[3,3,1024]{2,1,0:T(4,128)}, u32[]{:S(2)}) copy-start(f32[3,3,1024]{2,1,0:T(4,128)} %param.14) | copy-start | bytes 110596
  1.3 16.0 %collective-permute-start = (bf16[4,16,8,1024]{3,2,1,0:T(8,128)(2,1)S(1)}, bf16[4,16,8,1024]{3,2,1,0:T(8,128)(2,1)S(1)}, u32[]{:S(2)}, u32[]{:S(2)}) collective-permute-start(bf16[4,16,8,1024]{3,2,1,0:T(8,128)(2,1)S(1)} %pad_maximum_fusion.4), channel_id=1, source_target_pairs={{0,32},{32,64},{64,96},{96,128},{128,160},{160,192},{192,224},{224... | collective-permute-start | bytes 3145736 | tf_op jit(solution)/shard_map/ppermute | solution.py:15
  5.6 16.1 %collective-permute-start.1 = (bf16[4,16,8,1024]{3,2,1,0:T(8,128)(2,1)S(1)}, bf16[4,16,8,1024]{3,2,1,0:T(8,128)(2,1)S(1)}, u32[]{:S(2)}, u32[]{:S(2)}) collective-permute-start(bf16[4,16,8,1024]{3,2,1,0:T(8,128)(2,1)S(1)} %pad_maximum_fusion.4), channel_id=1, source_target_pairs={{32,0},{64,32},{96,64},{128,96},{160,128},{192,160},{224,192},{256... | collective-permute-start | bytes 3145736 | tf_op jit(solution)/shard_map/ppermute | solution.py:18
  21.7 3.4 copy-start.1
  25.1 559.7 %collective-permute-start.2 = (bf16[4,48,8,1024]{3,2,1,0:T(8,128)(2,1)}, bf16[4,48,8,1024]{3,2,1,0:T(8,128)(2,1)}, u32[]{:S(2)}, u32[]{:S(2)}) collective-permute-start(bf16[4,48,8,1024]{3,2,1,0:T(8,128)(2,1)} %pad_maximum_fusion.1), channel_id=1, source_target_pairs={{0,2},{1,3},{2,4},{3,5},{4,6},{5,7},{6,8},{7,9},{8,10},{9,11},{10,... | collective-permute-start | bytes 9437192 | tf_op jit(solution)/shard_map/ppermute | solution.py:26
  28.3 571.8 %collective-permute-start.3 = (bf16[4,48,8,1024]{3,2,1,0:T(8,128)(2,1)}, bf16[4,48,8,1024]{3,2,1,0:T(8,128)(2,1)}, u32[]{:S(2)}, u32[]{:S(2)}) collective-permute-start(bf16[4,48,8,1024]{3,2,1,0:T(8,128)(2,1)} %pad_maximum_fusion.1), channel_id=1, source_target_pairs={{0,1},{1,2},{2,3},{3,4},{4,5},{5,6},{6,7},{7,8},{8,9},{9,10},{10,1... | collective-permute-start | bytes 9437192 | tf_op jit(solution)/shard_map/ppermute | solution.py:26
  42.0 560.9 %collective-permute-start.4 = (bf16[4,48,8,1024]{3,2,1,0:T(8,128)(2,1)}, bf16[4,48,8,1024]{3,2,1,0:T(8,128)(2,1)}, u32[]{:S(2)}, u32[]{:S(2)}) collective-permute-start(bf16[4,48,8,1024]{3,2,1,0:T(8,128)(2,1)} %pad_maximum_fusion.1), channel_id=1, source_target_pairs={{1,0},{2,1},{3,2},{4,3},{5,4},{6,5},{7,6},{8,7},{9,8},{10,9},{11,1... | collective-permute-start | bytes 9437192 | tf_op jit(solution)/shard_map/ppermute | solution.py:26
  43.9 561.2 %collective-permute-start.5 = (bf16[4,48,8,1024]{3,2,1,0:T(8,128)(2,1)}, bf16[4,48,8,1024]{3,2,1,0:T(8,128)(2,1)}, u32[]{:S(2)}, u32[]{:S(2)}) collective-permute-start(bf16[4,48,8,1024]{3,2,1,0:T(8,128)(2,1)} %pad_maximum_fusion.1), channel_id=1, source_target_pairs={{2,0},{3,1},{4,2},{5,3},{6,4},{7,5},{8,6},{9,7},{10,8},{11,9},{12,... | collective-permute-start | bytes 9437192 | tf_op jit(solution)/shard_map/ppermute | solution.py:26
  48.0 7.2 %collective-permute-start.6 = (bf16[1,8,1024]{2,1,0:T(8,128)(2,1)S(1)}, bf16[1,8,1024]{2,1,0:T(8,128)(2,1)S(1)}, u32[]{:S(2)}, u32[]{:S(2)}) collective-permute-start(bf16[1,8,1024]{2,1,0:T(8,128)(2,1)S(1)} %get-tuple-element.88), channel_id=1, source_target_pairs={{0,32},{32,64},{64,96},{96,128},{128,160},{160,192},{192,224},{224... | collective-permute-start | bytes 49160 | tf_op jit(solution)/shard_map/ppermute | solution.py:15
  55.2 527.5 %collective-permute-start.7 = (bf16[1,8,1024]{2,1,0:T(8,128)(2,1)S(1)}, bf16[1,8,1024]{2,1,0:T(8,128)(2,1)S(1)}, u32[]{:S(2)}, u32[]{:S(2)}) collective-permute-start(bf16[1,8,1024]{2,1,0:T(8,128)(2,1)S(1)} %get-tuple-element.87), channel_id=1, source_target_pairs={{32,0},{64,32},{96,64},{128,96},{160,128},{192,160},{224,192},{256... | collective-permute-start | bytes 49160 | tf_op jit(solution)/shard_map/ppermute | solution.py:18
  582.9 77.3 %collective-permute-start.8 = (bf16[18,1,1024]{2,1,0:T(2,128)(2,1)S(1)}, bf16[18,1,1024]{2,1,0:T(2,128)(2,1)S(1)}, u32[]{:S(2)}, u32[]{:S(2)}) collective-permute-start(bf16[18,1,1024]{2,1,0:T(2,128)(2,1)S(1)} %get-tuple-element.85), channel_id=1, source_target_pairs={{0,1},{1,2},{2,3},{3,4},{4,5},{5,6},{6,7},{7,8},{8,9},{9,10},{10,1... | collective-permute-start | bytes 110600 | tf_op jit(solution)/shard_map/ppermute | solution.py:15
  584.8 75.4 %collective-permute-start.9 = (bf16[18,1,1024]{2,1,0:T(2,128)(2,1)S(1)}, bf16[18,1,1024]{2,1,0:T(2,128)(2,1)S(1)}, u32[]{:S(2)}, u32[]{:S(2)}) collective-permute-start(bf16[18,1,1024]{2,1,0:T(2,128)(2,1)S(1)} %get-tuple-element.86), channel_id=1, source_target_pairs={{1,0},{2,1},{3,2},{4,3},{5,4},{6,5},{7,6},{8,7},{9,8},{10,9},{11,1... | collective-permute-start | bytes 110600 | tf_op jit(solution)/shard_map/ppermute | solution.py:18
  600.1 2.3 copy-start.2
  607.4 6.0 copy-start.3
  613.4 46.9 %copy-start.5 = (f32[1024]{0:T(1024)S(1)}, f32[1024]{0:T(1024)}, u32[]{:S(2)}) copy-start(f32[1024]{0:T(1024)} %param.15) | copy-start | bytes 12292
where the time goes:
time: 663 us; the launch traced here: 662 us
  starting transfers between devices  567 us (86%)
  local copies, waits for them, and re-layouts  29.7 us (4%)
  matrix products  27.9 us (4%)
  waiting for transfers between devices  21.6 us (3%)
  other arithmetic  10.7 us (2%)
    ppermute x3, starting transfers between devices, with_halo(): lax.ppermute(lax.slice_in_dim(block, 0, width, axis=dim), axis, backward)  535 us
    ppermute x4, starting transfers between devices, passed_along(): return lax.ppermute(value, axis, pairs)  22.8 us
    dot_general x8, matrix products, one_head(): jnp.einsum('qd,kd->qk', query_head, key_head, preferred_element_type=jnp....  14.4 us
    dot_general x8, matrix products, one_head(): jnp.dot(weights_f.astype(jnp.bfloat16), value_head, preferred_element_typ...  13.5 us
  transfers between devices with their start and end apart: 10, of which 3 were waited for; matrix products, arithmetic and copies ran while one was open for 9% of the time, Pallas kernels for 0%

commit v1 on v0

v1 whole, which is shorter than its diff:
```python
import functools

import jax
import jax.numpy as jnp
from jax import lax
from jax.experimental import pallas as pl
from jax.experimental.pallas import tpu as pltpu
from jax.sharding import PartitionSpec as P

MESH = pl.DeviceIdType.MESH
HD = 128
WIN = 32
HALF = WIN // 2
ROWS = 16
COLS = 8
TILE = ROWS * COLS
HEADS = 8
GROUP = HEADS // 2
KEYS = 3 * TILE
EDGE = 2 * ROWS
LOG2E = 1.4426950408889634
MASKED = -1e30


def iota(shape, dim):
    return lax.broadcasted_iota(jnp.int32, shape, dim)


def row_bias(chip, chips, t):
    q_row = iota((TILE, KEYS), 0) // COLS
    k_row = iota((TILE, KEYS), 1) // COLS - ROWS
    frame_row = k_row + (2 * chip + t) * ROWS
    delta = k_row - q_row
    return (delta >= -HALF) & (delta < HALF) & (frame_row >= 0) & (frame_row < chips * 2 * ROWS)


def kernel(
    chips, strips, q_ref, kc_ref, kn_ref, vc_ref, vn_ref, cw_ref, cb_ref, out_ref,
    src, qsrc, kv, qb, own_bias, far_bias, own_o, own_s, far_send, far_recv, stat_send, stat_recv, stage,
    load_sem, qload_sem, local_sem, qlocal_sem,
    z_send, y_send, sib_send, relay_send, q_send, qsib_send, o_send, s_send, out_send, out_local,
    kv_recv, q_recv, o_recv, s_recv, out_recv,
):
    ht = lax.axis_index("ht")
    wt = lax.axis_index("wt")
    chip, core = ht // 2, ht % 2
    strip, half = wt // 2, wt % 2
    other = 1 - core
    far = wt + 1 - 2 * half
    has_up, has_down = chip > 0, chip < chips - 1
    has_left, has_right = strip > 0, strip < strips - 1

    def remote(source, target, send_sem, recv_sem, to_ht, to_wt):
        return pltpu.make_async_remote_copy(
            src_ref=source, dst_ref=target, send_sem=send_sem, recv_sem=recv_sem,
            device_id={"ht": to_ht, "wt": to_wt}, device_id_type=MESH,
        )

    inputs = (kc_ref, kn_ref, vc_ref, vn_ref)
    order = [g * GROUP + i for i in range(GROUP) for g in range(2)]

    def load(head, a):
        lanes = pl.ds(head * HD, HD)
        return pltpu.make_async_copy(inputs[a].at[:, lanes], src.at[head, a], load_sem.at[head, a])

    def qload(head):
        return pltpu.make_async_copy(q_ref.at[:, pl.ds(head * HD, HD)], qsrc.at[head], qload_sem.at[head])

    for head in order:
        for a in range(4):
            load(head, a).start()
        qload(head).start()

    barrier = pltpu.get_barrier_semaphore()

    def greet(to_ht, to_wt):
        pl.semaphore_signal(barrier, inc=1, device_id={"ht": to_ht, "wt": to_wt}, device_id_type=MESH)

    greet(2 * chip + other, wt)
    for c in range(2):
        greet(2 * chip + c, far)

        @pl.when(has_up)
        def _():
            greet(2 * (chip - 1) + c, wt)

        @pl.when(has_down)
        def _():
            greet(2 * (chip + 1) + c, wt)

        @pl.when(has_left)
        def _():
            greet(2 * chip + c, wt - 2)

        @pl.when(has_right)
        def _():
            greet(2 * chip + c, wt + 2)

    def clear(s, r):
        @pl.loop(0, GROUP)
        def _(i):
            kv[i, s, r] = jnp.zeros((4, TILE, HD), jnp.bfloat16)

    @pl.when(jnp.logical_not(has_left))
    def _():
        for r in range(4):
            clear(0, r)

    @pl.when(jnp.logical_not(has_right))
    def _():
        for r in range(4):
            clear(2, r)

    @pl.when(jnp.logical_not(has_up))
    def _():
        for s in range(3):
            clear(s, 0)

    @pl.when(jnp.logical_not(has_down))
    def _():
        for s in range(3):
            clear(s, 3)

    for head in order:
        for a in range(4):
            load(head, a).wait()
        qload(head).wait()

    greeted = 3 + 2 * (
        has_up.astype(jnp.int32) + has_down.astype(jnp.int32) + has_left.astype(jnp.int32) + has_right.astype(jnp.int32)
    )
    pl.semaphore_wait(barrier, greeted)

    sends_z = jnp.where(core == 1, chip < chips - 1, chip > 0)
    z_chip = jnp.where(core == 1, jnp.minimum(chip + 1, chips - 1), jnp.maximum(chip - 1, 0))
    z_slot = 3 * other

    def z_copy(i, c):
        return remote(
            src.at[c * GROUP + i], kv.at[i, 1, z_slot], z_send.at[i, c], kv_recv.at[i, 1, z_slot], 2 * z_chip + c, wt
        )

    def sib_copy(i):
        return remote(
            src.at[other * GROUP + i], kv.at[i, 1, 1 + core], sib_send.at[i], kv_recv.at[i, 1, 1 + core],
            2 * chip + other, wt,
        )

    def own_copy(i):
        return pltpu.make_async_copy(src.at[core * GROUP + i], kv.at[i, 1, 1 + core], local_sem.at[i])

    sides = ((has_left, -2, 2), (has_right, 2, 0))

    def y_copy(i, d, c):
        _, step, s = sides[d]
        return remote(
            src.at[c * GROUP + i], kv.at[i, s, 1 + core], y_send.at[i, d, c], kv_recv.at[i, s, 1 + core],
            2 * chip + c, wt + step,
        )

    def relay_copy(i, d, n):
        _, step, s = sides[d]
        return remote(
            kv.at[i, 1, 3 * n], kv.at[i, s, 3 * n], relay_send.at[i, d, n], kv_recv.at[i, s, 3 * n], ht, wt + step
        )

    def q_copy(i, c):
        return remote(
            qsrc.at[c * GROUP + i], qb.at[i, 1, core], q_send.at[i, c], q_recv.at[i, 1, core], 2 * chip + c, far
        )

    def qsib_copy(i):
        return remote(
            qsrc.at[other * GROUP + i], qb.at[i, 0, core], qsib_send.at[i], q_recv.at[i, 0, core],
            2 * chip + other, wt,
        )

    def qown_copy(i):
        return pltpu.make_async_copy(qsrc.at[core * GROUP + i], qb.at[i, 0, core], qlocal_sem.at[i])

    def kv_arrived(i, s, r):
        pltpu.make_async_copy(src.at[0], kv.at[i, s, r], kv_recv.at[i, s, r]).wait()

    for i in range(GROUP):
        @pl.when(sends_z)
        def _():
            for c in range(2):
                z_copy(i, c).start()

    for i in range(GROUP):
        sib_copy(i).start()
        own_copy(i).start()
        qsib_copy(i).start()
        qown_copy(i).start()
        for c in range(2):
            q_copy(i, c).start()

    ends = (has_up, has_down)
    for i in range(GROUP):
        for d in range(2):
            @pl.when(sides[d][0])
            def _():
                for c in range(2):
                    y_copy(i, d, c).start()

        if i == 0:
            for t in range(2):
                rows = row_bias(chip, chips, t)
                q_col = iota((TILE, KEYS), 0) % COLS
                k_col = iota((TILE, KEYS), 1) % COLS
                for s in range(3):
                    delta = k_col - q_col + (s - 1) * 2 * COLS
                    inside = (strip + s - 1 >= 0) & (strip + s - 1 < strips)
                    ok = rows & (delta >= -HALF) & (delta < HALF)
                    own_bias[t, s] = jnp.where(ok & inside, 0.0, MASKED)
                for n in range(2):
                    at = strip + n - half
                    far_bias[t, n] = jnp.where(rows & (at >= 0) & (at < strips), 0.0, MASKED)

        for n in range(2):
            @pl.when(ends[n])
            def _():
                kv_arrived(i, 1, 3 * n)
                for d in range(2):
                    @pl.when(sides[d][0])
                    def _():
                        relay_copy(i, d, n).start()

    eye = iota((TILE, TILE), 0) == iota((TILE, TILE), 1)

    def attend(q, i, t, blocks):
        scores = []
        for s, bias in blocks:
            for f in range(2):
                k = kv[i, s, pl.ds(t, 3), f].reshape(KEYS, HD)
                dots = lax.dot_general(q, k, (((1,), (1,)), ((), ())), preferred_element_type=jnp.float32)
                scores.append(dots * (HD**-0.5 * LOG2E) + bias[...])
        top = functools.reduce(jnp.maximum, scores)
        top = jnp.max(top, axis=1, keepdims=True)
        total = jnp.zeros((TILE, KEYS), jnp.float32)
        acc = jnp.zeros((TILE, HD), jnp.float32)
        n = 0
        for s, _ in blocks:
            for f in range(2):
                weights = jnp.exp2(scores[n] - top)
                total = total + weights
                v = kv[i, s, pl.ds(t, 3), 2 + f].reshape(KEYS, HD)
                acc = acc + jnp.dot(weights.astype(jnp.bfloat16), v, preferred_element_type=jnp.float32)
                n += 1
        total = jnp.sum(total, axis=1, keepdims=True)
        return acc * (1.0 / total), top + jnp.log2(total)

    def taps(i):
        lanes = pl.ds(pl.multiple_of((core * GROUP + i) * HD, HD), HD)
        return [[cw_ref[pl.ds(3 * a + b, 1), lanes] for b in range(3)] for a in range(3)], cb_ref[:, lanes]

    def edges(i, t):
        weight, _ = taps(i)
        pick = iota((3 * ROWS, KEYS), 0)
        key = iota((3 * ROWS, KEYS), 1)
        wanted = (ROWS - 1 + pick % ROWS + pick // ROWS) * COLS
        parts = []
        for n, col, b in ((0, COLS - 1, 0), (1, 0, 2)):
            v = kv[i, 1 - half + n, pl.ds(t, 3), 3].reshape(KEYS, HD)
            chosen = jnp.where(key == wanted + col, 1.0, 0.0).astype(jnp.bfloat16)
            picked = jnp.dot(chosen, v, preferred_element_type=jnp.float32)
            parts.append(sum(picked[a * ROWS : (a + 1) * ROWS] * weight[a][b] for a in range(3)))
        return jnp.concatenate(parts, axis=0).astype(jnp.bfloat16)

    def conv(i, t):
        weight, bias = taps(i)
        v = kv[i, 1, pl.ds(t, 3), 3].reshape(KEYS, HD).astype(jnp.float32)
        rows = [v[TILE + (a - 1) * COLS : 2 * TILE + (a - 1) * COLS] for a in range(3)]
        left, here, right = (sum(rows[a] * weight[a][b] for a in range(3)) for b in range(3))
        col = iota((TILE, HD), 0) % COLS
        left = jnp.where(col == 0, 0.0, pltpu.roll(left, 1, 0))
        right = jnp.where(col == COLS - 1, 0.0, pltpu.roll(right, TILE - 1, 0))
        return here + left + right + bias

    def o_copy(i):
        return remote(far_send.at[i], far_recv.at[i], o_send.at[i], o_recv.at[i], ht, far)

    def s_copy(i):
        return remote(stat_send.at[i], stat_recv.at[i], s_send.at[i], s_recv.at[i], ht, far)

    def wait_inputs(i):
        own_copy(i).wait()
        qown_copy(i).wait()
        kv_arrived(i, 1, 1 + other)
        pltpu.make_async_copy(qsrc.at[0], qb.at[i, 0, other], q_recv.at[i, 0, other]).wait()
        for t in range(2):
            pltpu.make_async_copy(qsrc.at[0], qb.at[i, 1, t], q_recv.at[i, 1, t]).wait()
        for valid, s in ((has_left, 0), (has_right, 2)):
            @pl.when(valid)
            def _():
                kv_arrived(i, s, 1)
                kv_arrived(i, s, 2)

                @pl.when(has_up)
                def _():
                    kv_arrived(i, s, 0)

                @pl.when(has_down)
                def _():
                    kv_arrived(i, s, 3)

    @pl.loop(0, GROUP)
    def _(i):
        wait_inputs(i)

        @pl.loop(0, 2)
        def _(t):
            o, s = attend(qb[i, 1, t], i, t, [(1 - half + n, far_bias.at[t, n]) for n in range(2)])
            far_send[i, t, :TILE] = o.astype(jnp.bfloat16)
            far_send[i, t, TILE:] = edges(i, t)
            stat_send[i, pl.ds(t, 1)] = jnp.sum(jnp.where(eye, s, 0.0), axis=0, keepdims=True)

        o_copy(i).start()
        s_copy(i).start()

        @pl.loop(0, 2)
        def _(t):
            o, s = attend(qb[i, 0, t], i, t, [(n, own_bias.at[t, n]) for n in range(3)])
            own_o[i, t] = o
            own_s[i, t] = jnp.broadcast_to(s, (TILE, HD))

    def out_lanes(i):
        return out_ref.at[:, pl.ds(pl.multiple_of((core * GROUP + i) * HD, HD), HD)]

    def out_own(i):
        return pltpu.make_async_copy(stage.at[i, core], out_lanes(i), out_local.at[i])

    def out_sib(i):
        return remote(stage.at[i, other], out_lanes(i), out_send.at[i], out_recv.at[i], 2 * chip + other, wt)

    @pl.loop(0, GROUP)
    def _(i):
        o_copy(i).wait_recv()
        s_copy(i).wait_recv()

        @pl.loop(0, 2)
        def _(t):
            far_s = jnp.sum(jnp.where(eye, stat_recv[i, pl.ds(t, 1)], 0.0), axis=1, keepdims=True)
            shift = far_s - own_s[i, t]
            own_w = 1.0 / (1.0 + jnp.exp2(shift))
            far_w = 1.0 / (1.0 + jnp.exp2(-shift))
            place = iota((TILE, EDGE), 0)
            edge = iota((TILE, EDGE), 1)
            spot = (edge % ROWS) * COLS + (edge // ROWS) * (COLS - 1)
            spread = jnp.where(place == spot, 1.0, 0.0).astype(jnp.bfloat16)
            edge_part = jnp.dot(spread, far_recv[i, t, TILE:], preferred_element_type=jnp.float32)
            mixed = own_o[i, t] * own_w + far_recv[i, t, :TILE].astype(jnp.float32) * far_w
            stage[i, t] = (mixed + (conv(i, t) + edge_part)).astype(jnp.bfloat16)

        out_sib(i).start()
        out_own(i).start()

    for i in range(GROUP):
        @pl.when(sends_z)
        def _():
            for c in range(2):
                z_copy(i, c).wait_send()

        sib_copy(i).wait_send()
        qsib_copy(i).wait_send()
        for c in range(2):
            q_copy(i, c).wait_send()
        for d in range(2):
            @pl.when(sides[d][0])
            def _():
                for c in range(2):
                    y_copy(i, d, c).wait_send()
                for n in range(2):
                    @pl.when(ends[n])
                    def _():
                        relay_copy(i, d, n).wait_send()

        o_copy(i).wait_send()
        s_copy(i).wait_send()
        out_sib(i).wait_send()
        out_own(i).wait()
        pltpu.make_async_copy(
            stage.at[i, 0],
            out_ref.at[:, pl.ds(pl.multiple_of((other * GROUP + i) * HD, HD), HD)],
            out_recv.at[i],
        ).wait()


def shards(chips, strips, queries, keys_new, values_new, keys_cache, values_cache, conv_weight, conv_bias):
    rows, cols, channels = queries.shape
    flat = [x.reshape(TILE, channels) for x in (queries, keys_cache, keys_new, values_cache, values_new)]
    any_spec = pl.BlockSpec(memory_space=pl.ANY)
    vmem_spec = pl.BlockSpec(memory_space=pltpu.VMEM)
    bf16, f32 = jnp.bfloat16, jnp.float32
    dma = pltpu.SemaphoreType.DMA
    out = pl.pallas_call(
        functools.partial(kernel, chips, strips),
        out_shape=jax.ShapeDtypeStruct((TILE, channels), bf16),
        in_specs=[any_spec] * 5 + [vmem_spec] * 2,
        out_specs=any_spec,
        scratch_shapes=[
            pltpu.VMEM((HEADS, 4, TILE, HD), bf16),
            pltpu.VMEM((HEADS, TILE, HD), bf16),
            pltpu.VMEM((GROUP, 3, 4, 4, TILE, HD), bf16),
            pltpu.VMEM((GROUP, 2, 2, TILE, HD), bf16),
            pltpu.VMEM((2, 3, TILE, KEYS), f32),
            pltpu.VMEM((2, 2, TILE, KEYS), f32),
            pltpu.VMEM((GROUP, 2, TILE, HD), f32),
            pltpu.VMEM((GROUP, 2, TILE, HD), f32),
            pltpu.VMEM((GROUP, 2, TILE + EDGE, HD), bf16),
            pltpu.VMEM((GROUP, 2, TILE + EDGE, HD), bf16),
            pltpu.VMEM((GROUP, 2, HD), f32),
            pltpu.VMEM((GROUP, 2, HD), f32),
            pltpu.VMEM((GROUP, 2, TILE, HD), bf16),
            dma((HEADS, 4)), dma((HEADS,)), dma((GROUP,)), dma((GROUP,)),
            dma((GROUP, 2)), dma((GROUP, 2, 2)), dma((GROUP,)), dma((GROUP, 2, 2)), dma((GROUP, 2)), dma((GROUP,)),
            dma((GROUP,)), dma((GROUP,)), dma((GROUP,)), dma((GROUP,)),
            dma((GROUP, 3, 4)), dma((GROUP, 2, 2)), dma((GROUP,)), dma((GROUP,)), dma((GROUP,)),
        ],
        compiler_params=pltpu.CompilerParams(
            collective_id=0, has_side_effects=True, vmem_limit_bytes=56 << 20
        ),
    )(*flat, conv_weight.reshape(9, channels), conv_bias.reshape(1, channels))
    return out.reshape(rows, cols, channels)


def solution(mesh):
    placed = (
        P("ht", "wt", None),
        P("ht", "wt", None),
        P("ht", "wt", None),
        P(None, "ht", "wt", None),
        P(None, "ht", "wt", None),
        P(),
        P(),
    )
    body = functools.partial(shards, mesh.shape["ht"] // 2, mesh.shape["wt"] // 2)
    return jax.shard_map(body, mesh=mesh, in_specs=placed, out_specs=P("ht", "wt", None), check_vma=False)
```

time: 663 us -> 90.8 us (0.14)
  the two profiles are of different devices: /device:TPU:47 before, /device:TPU:1 now
where the time goes in v1:
time: 90.8 us; the launch traced here: 89.1 us
  Pallas kernels  86 us (95%)
  local copies, waits for them, and re-layouts  3.12 us (3%)
    pallas_call x1, Pallas kernels, shards(): pl.pallas_call(functools.partial(kernel, chips, strips), out_shape=jax.Sh...  86 us

profile of v1, /device:TPU:1, one launch (start us, length us, event | category | flops | bytes accessed | tf_op | source)
XLA Modules:
  0.0 89.1 jit_solution(9689882227784956962)
XLA Ops:
  0.0 1.4 %reshape.29.cw_ref = f32[9,1024]{1,0:T(8,128)} reshape(f32[3,3,1024]{2,1,0:T(4,128)} %param.12) | data formatting | bytes 73728 | tf_op jit(solution)/shard_map/reshape | solution.py:423
  1.4 86.0 %shard_map.73 = bf16[128,1024]{1,0:T(8,128)(2,1)} custom-call(bf16[128,1024]{1,0:T(8,128)(2,1)} %bitcast.8, bf16[128,1024]{1,0:T(8,128)(2,1)} %bitcast.9, bf16[128,1024]{1,0:T(8,128)(2,1)} %bitcast.10, bf16[128,1024]{1,0:T(8,128)(2,1)} %bitcast.11, bf16[128,1024]{1,0:T(8,128)(2,1)} %bitcast.12, f32[9,1024]{1,0:T(8,128)} %reshape.29.cw_ref, f32[1,1024]{1,0:T(1,128)} %bitcast.13), custom_call_target="tpu_custom_call" | custom-call | tf_op jit(solution)/shard_map/pallas_call | solution.py:396
  87.5 1.7 %copy.9 = bf16[16,8,1024]{2,1,0:T(8,128)(2,1)} copy(bf16[16,8,1024]{2,1,0:T(8,128)(2,1)} %bitcast.7) | data formatting | bytes 524288

commit v2 on v1

--- a/solution.py
+++ b/solution.py
@@ -36,10 +36,10 @@
 
 def kernel(
     chips, strips, q_ref, kc_ref, kn_ref, vc_ref, vn_ref, cw_ref, cb_ref, out_ref,
-    src, qsrc, kv, qb, own_bias, far_bias, own_o, own_s, far_send, far_recv, stat_send, stat_recv, stage,
+    src, qsrc, kv, qb, own_bias, far_bias, own, sib_in, far_send, far_recv, stat_send, stat_recv,
     load_sem, qload_sem, local_sem, qlocal_sem,
-    z_send, y_send, sib_send, relay_send, q_send, qsib_send, o_send, s_send, out_send, out_local,
-    kv_recv, q_recv, o_recv, s_recv, out_recv,
+    z_send, y_send, sib_send, relay_send, q_send, qsib_send, o_send, s_send, own_send,
+    kv_recv, q_recv, o_recv, s_recv, own_recv,
 ):
     ht = lax.axis_index("ht")
     wt = lax.axis_index("wt")
@@ -66,36 +66,36 @@
     def qload(head):
         return pltpu.make_async_copy(q_ref.at[:, pl.ds(head * HD, HD)], qsrc.at[head], qload_sem.at[head])
 
+    barrier = pltpu.get_barrier_semaphore()
+
+    def greet(to_ht, to_wt):
+        pl.semaphore_signal(barrier, inc=1, device_id={"ht": to_ht, "wt": to_wt}, device_id_type=MESH)
+
+    greet(2 * chip + other, wt)
+    for c in range(2):
+        greet(2 * chip + c, far)
+
+        @pl.when(has_up)
+        def _():
+            greet(2 * (chip - 1) + c, wt)
+
+        @pl.when(has_down)
+        def _():
+            greet(2 * (chip + 1) + c, wt)
+
+        @pl.when(has_left)
+        def _():
+            greet(2 * chip + c, wt - 2)
+
+        @pl.when(has_right)
+        def _():
+            greet(2 * chip + c, wt + 2)
+
     for head in order:
         for a in range(4):
             load(head, a).start()
         qload(head).start()
 
-    barrier = pltpu.get_barrier_semaphore()
-
-    def greet(to_ht, to_wt):
-        pl.semaphore_signal(barrier, inc=1, device_id={"ht": to_ht, "wt": to_wt}, device_id_type=MESH)
-
-    greet(2 * chip + other, wt)
-    for c in range(2):
-        greet(2 * chip + c, far)
-
-        @pl.when(has_up)
-        def _():
-            greet(2 * (chip - 1) + c, wt)
-
-        @pl.when(has_down)
-        def _():
-            greet(2 * (chip + 1) + c, wt)
-
-        @pl.when(has_left)
-        def _():
-            greet(2 * chip + c, wt - 2)
-
-        @pl.when(has_right)
-        def _():
-            greet(2 * chip + c, wt + 2)
-
     def clear(s, r):
         @pl.loop(0, GROUP)
         def _(i):
@@ -186,14 +186,19 @@
         def _():
             for c in range(2):
                 z_copy(i, c).start()
+
+        if i > 0:
+            for c in range(2):
+                q_copy(i - 1, c).start()
+
+    for c in range(2):
+        q_copy(GROUP - 1, c).start()
 
     for i in range(GROUP):
         sib_copy(i).start()
         own_copy(i).start()
         qsib_copy(i).start()
         qown_copy(i).start()
-        for c in range(2):
-            q_copy(i, c).start()
 
     ends = (has_up, has_down)
     for i in range(GROUP):
@@ -252,7 +257,7 @@
 
     def taps(i):
         lanes = pl.ds(pl.multiple_of((core * GROUP + i) * HD, HD), HD)
-        return [[cw_ref[pl.ds(3 * a + b, 1), lanes] for b in range(3)] for a in range(3)], cb_ref[:, lanes]
+        return [[cw_ref[a, pl.ds(b, 1), lanes] for b in range(3)] for a in range(3)], cb_ref[:, lanes]
 
     def edges(i, t):
         weight, _ = taps(i)
@@ -277,11 +282,18 @@
         right = jnp.where(col == COLS - 1, 0.0, pltpu.roll(right, TILE - 1, 0))
         return here + left + right + bias
 
-    def o_copy(i):
-        return remote(far_send.at[i], far_recv.at[i], o_send.at[i], o_recv.at[i], ht, far)
-
-    def s_copy(i):
-        return remote(stat_send.at[i], stat_recv.at[i], s_send.at[i], s_recv.at[i], ht, far)
+    def o_copy(i, t):
+        return remote(
+            far_send.at[i, t], far_recv.at[core, i], o_send.at[i, t], o_recv.at[core, i], 2 * chip + t, far
+        )
+
+    def s_copy(i, t):
+        return remote(
+            stat_send.at[i, t], stat_recv.at[core, i], s_send.at[i, t], s_recv.at[core, i], 2 * chip + t, far
+        )
+
+    def own_part_copy(i):
+        return remote(own.at[i, other], sib_in.at[i], own_send.at[i], own_recv.at[i], 2 * chip + other, wt)
 
     def wait_inputs(i):
         own_copy(i).wait()
@@ -313,47 +325,41 @@
             o, s = attend(qb[i, 1, t], i, t, [(1 - half + n, far_bias.at[t, n]) for n in range(2)])
             far_send[i, t, :TILE] = o.astype(jnp.bfloat16)
             far_send[i, t, TILE:] = edges(i, t)
-            stat_send[i, pl.ds(t, 1)] = jnp.sum(jnp.where(eye, s, 0.0), axis=0, keepdims=True)
-
-        o_copy(i).start()
-        s_copy(i).start()
+            stat_send[i, t] = jnp.sum(jnp.where(eye, s, 0.0), axis=0, keepdims=True)
+            s_copy(i, t).start()
+            o_copy(i, t).start()
 
         @pl.loop(0, 2)
         def _(t):
             o, s = attend(qb[i, 0, t], i, t, [(n, own_bias.at[t, n]) for n in range(3)])
-            own_o[i, t] = o
-            own_s[i, t] = jnp.broadcast_to(s, (TILE, HD))
-
-    def out_lanes(i):
-        return out_ref.at[:, pl.ds(pl.multiple_of((core * GROUP + i) * HD, HD), HD)]
-
-    def out_own(i):
-        return pltpu.make_async_copy(stage.at[i, core], out_lanes(i), out_local.at[i])
-
-    def out_sib(i):
-        return remote(stage.at[i, other], out_lanes(i), out_send.at[i], out_recv.at[i], 2 * chip + other, wt)
+            own[i, t, 0] = o
+            own[i, t, 1] = conv(i, t)
+            own[i, t, 2] = jnp.broadcast_to(s, (TILE, HD))
+
+        own_part_copy(i).start()
+
+    def complete(i, g, mine):
+        pltpu.make_async_copy(stat_send.at[i, 0], stat_recv.at[g, i], s_recv.at[g, i]).wait()
+        far_s = jnp.sum(jnp.where(eye, stat_recv[g, i], 0.0), axis=1, keepdims=True)
+        shift = far_s - mine[2]
+        own_w = 1.0 / (1.0 + jnp.exp2(shift))
+        far_w = 1.0 / (1.0 + jnp.exp2(-shift))
+        here = mine[0] * own_w + mine[1]
+        place = iota((TILE, EDGE), 0)
+        edge = iota((TILE, EDGE), 1)
+        spot = (edge % ROWS) * COLS + (edge // ROWS) * (COLS - 1)
+        spread = jnp.where(place == spot, 1.0, 0.0).astype(jnp.bfloat16)
+        pltpu.make_async_copy(far_send.at[i, 0], far_recv.at[g, i], o_recv.at[g, i]).wait()
+        edge_part = jnp.dot(spread, far_recv[g, i, TILE:], preferred_element_type=jnp.float32)
+        there = far_recv[g, i, :TILE].astype(jnp.float32) * far_w
+        lanes = pl.ds(pl.multiple_of((g * GROUP + i) * HD, HD), HD)
+        out_ref[:, lanes] = (here + there + edge_part).astype(jnp.bfloat16)
 
     @pl.loop(0, GROUP)
     def _(i):
-        o_copy(i).wait_recv()
-        s_copy(i).wait_recv()
-
-        @pl.loop(0, 2)
-        def _(t):
-            far_s = jnp.sum(jnp.where(eye, stat_recv[i, pl.ds(t, 1)], 0.0), axis=1, keepdims=True)
-            shift = far_s - own_s[i, t]
-            own_w = 1.0 / (1.0 + jnp.exp2(shift))
-            far_w = 1.0 / (1.0 + jnp.exp2(-shift))
-            place = iota((TILE, EDGE), 0)
-            edge = iota((TILE, EDGE), 1)
-            spot = (edge % ROWS) * COLS + (edge // ROWS) * (COLS - 1)
-            spread = jnp.where(place == spot, 1.0, 0.0).astype(jnp.bfloat16)
-            edge_part = jnp.dot(spread, far_recv[i, t, TILE:], preferred_element_type=jnp.float32)
-            mixed = own_o[i, t] * own_w + far_recv[i, t, :TILE].astype(jnp.float32) * far_w
-            stage[i, t] = (mixed + (conv(i, t) + edge_part)).astype(jnp.bfloat16)
-
-        out_sib(i).start()
-        out_own(i).start()
+        pltpu.make_async_copy(own.at[i, 0], sib_in.at[i], own_recv.at[i]).wait()
+        complete(i, core, own.at[i, core])
+        complete(i, other, sib_in.at[i])
 
     for i in range(GROUP):
         @pl.when(sends_z)
@@ -375,15 +381,10 @@
                     def _():
                         relay_copy(i, d, n).wait_send()
 
-        o_copy(i).wait_send()
-        s_copy(i).wait_send()
-        out_sib(i).wait_send()
-        out_own(i).wait()
-        pltpu.make_async_copy(
-            stage.at[i, 0],
-            out_ref.at[:, pl.ds(pl.multiple_of((other * GROUP + i) * HD, HD), HD)],
-            out_recv.at[i],
-        ).wait()
+        for t in range(2):
+            o_copy(i, t).wait_send()
+            s_copy(i, t).wait_send()
+        own_part_copy(i).wait_send()
 
 
 def shards(chips, strips, queries, keys_new, values_new, keys_cache, values_cache, conv_weight, conv_bias):
@@ -395,9 +396,9 @@
     dma = pltpu.SemaphoreType.DMA
     out = pl.pallas_call(
         functools.partial(kernel, chips, strips),
-        out_shape=jax.ShapeDtypeStruct((TILE, channels), bf16),
+        out_shape=pltpu.VMEM((TILE, channels), bf16),
         in_specs=[any_spec] * 5 + [vmem_spec] * 2,
-        out_specs=any_spec,
+        out_specs=vmem_spec,
         scratch_shapes=[
             pltpu.VMEM((HEADS, 4, TILE, HD), bf16),
             pltpu.VMEM((HEADS, TILE, HD), bf16),
@@ -405,22 +406,21 @@
             pltpu.VMEM((GROUP, 2, 2, TILE, HD), bf16),
             pltpu.VMEM((2, 3, TILE, KEYS), f32),
             pltpu.VMEM((2, 2, TILE, KEYS), f32),
-            pltpu.VMEM((GROUP, 2, TILE, HD), f32),
-            pltpu.VMEM((GROUP, 2, TILE, HD), f32),
+            pltpu.VMEM((GROUP, 2, 3, TILE, HD), f32),
+            pltpu.VMEM((GROUP, 3, TILE, HD), f32),
             pltpu.VMEM((GROUP, 2, TILE + EDGE, HD), bf16),
-            pltpu.VMEM((GROUP, 2, TILE + EDGE, HD), bf16),
-            pltpu.VMEM((GROUP, 2, HD), f32),
-            pltpu.VMEM((GROUP, 2, HD), f32),
-            pltpu.VMEM((GROUP, 2, TILE, HD), bf16),
+            pltpu.VMEM((2, GROUP, TILE + EDGE, HD), bf16),
+            pltpu.VMEM((GROUP, 2, 1, HD), f32),
+            pltpu.VMEM((2, GROUP, 1, HD), f32),
             dma((HEADS, 4)), dma((HEADS,)), dma((GROUP,)), dma((GROUP,)),
             dma((GROUP, 2)), dma((GROUP, 2, 2)), dma((GROUP,)), dma((GROUP, 2, 2)), dma((GROUP, 2)), dma((GROUP,)),
-            dma((GROUP,)), dma((GROUP,)), dma((GROUP,)), dma((GROUP,)),
-            dma((GROUP, 3, 4)), dma((GROUP, 2, 2)), dma((GROUP,)), dma((GROUP,)), dma((GROUP,)),
+            dma((GROUP, 2)), dma((GROUP, 2)), dma((GROUP,)),
+            dma((GROUP, 3, 4)), dma((GROUP, 2, 2)), dma((2, GROUP)), dma((2, GROUP)), dma((GROUP,)),
         ],
         compiler_params=pltpu.CompilerParams(
             collective_id=0, has_side_effects=True, vmem_limit_bytes=56 << 20
         ),
-    )(*flat, conv_weight.reshape(9, channels), conv_bias.reshape(1, channels))
+    )(*flat, conv_weight, conv_bias.reshape(1, channels))
     return out.reshape(rows, cols, channels)
 
 

time: 90.8 us -> 83.9 us (0.924); the launches traced: 89.1 us -> 83.7 us
  Pallas kernels: 86 us -> 82.9 us
  local copies, waits for them, and re-layouts: 3.12 us -> 0.71 us
    pallas_call x1, Pallas kernels: 86 us -> 82.9 us  [shards(): pl.pallas_call(functools.partial(kernel, chips, strips), out_shape=pltpu....]
    reshape x1 -> x0, local copies, waits for them, and re-layouts: 1.45 us -> none  [shards(): conv_weight.reshape(9, channels)]
    unnamed x1, local copies, waits for them, and re-layouts: 1.67 us -> 0.71 us
where the time goes in v2:
time: 83.9 us; the launch traced here: 83.7 us
  Pallas kernels  82.9 us (99%)
    pallas_call x1, Pallas kernels, shards(): pl.pallas_call(functools.partial(kernel, chips, strips), out_shape=pltpu....  82.9 us

profile of v2, /device:TPU:1, one launch (start us, length us, event | category | flops | bytes accessed | tf_op | source)
XLA Modules:
  0.0 83.7 jit_solution(2422553040757713255)
XLA Ops:
  0.0 82.9 %shard_map.73 = bf16[128,1024]{1,0:T(8,128)(2,1)S(1)} custom-call(bf16[128,1024]{1,0:T(8,128)(2,1)} %bitcast.8, bf16[128,1024]{1,0:T(8,128)(2,1)} %bitcast.9, bf16[128,1024]{1,0:T(8,128)(2,1)} %bitcast.10, bf16[128,1024]{1,0:T(8,128)(2,1)} %bitcast.11, bf16[128,1024]{1,0:T(8,128)(2,1)} %bitcast.12, f32[3,3,1024]{2,1,0:T(4,128)} %cw_ref.1, f32[1,1024]{1,0:T(1,128)} %bitcast.13), custom_call_target="tpu_custom_call" | custom-call | tf_op jit(solution)/shard_map/pallas_call | solution.py:397
  83.0 0.7 copy.9

commit v3 on v2

--- a/solution.py
+++ b/solution.py
@@ -121,10 +121,24 @@
         for s in range(3):
             clear(s, 3)
 
-    for head in order:
-        for a in range(4):
-            load(head, a).wait()
-        qload(head).wait()
+    for t in range(2):
+        rows = row_bias(chip, chips, t)
+        q_col = iota((TILE, KEYS), 0) % COLS
+        k_col = iota((TILE, KEYS), 1) % COLS
+        for s in range(3):
+            delta = k_col - q_col + (s - 1) * 2 * COLS
+            inside = (strip + s - 1 >= 0) & (strip + s - 1 < strips)
+            ok = rows & (delta >= -HALF) & (delta < HALF)
+            own_bias[t, s] = jnp.where(ok & inside, 0.0, MASKED)
+        for n in range(2):
+            at = strip + n - half
+            far_bias[t, n] = jnp.where(rows & (at >= 0) & (at < strips), 0.0, MASKED)
+
+    def loaded(i):
+        for head in (i, GROUP + i):
+            for a in range(4):
+                load(head, a).wait()
+            qload(head).wait()
 
     greeted = 3 + 2 * (
         has_up.astype(jnp.int32) + has_down.astype(jnp.int32) + has_left.astype(jnp.int32) + has_right.astype(jnp.int32)
@@ -181,47 +195,51 @@
     def kv_arrived(i, s, r):
         pltpu.make_async_copy(src.at[0], kv.at[i, s, r], kv_recv.at[i, s, r]).wait()
 
-    for i in range(GROUP):
+    def send_z(i):
         @pl.when(sends_z)
         def _():
             for c in range(2):
                 z_copy(i, c).start()
 
-        if i > 0:
-            for c in range(2):
-                q_copy(i - 1, c).start()
-
-    for c in range(2):
-        q_copy(GROUP - 1, c).start()
-
-    for i in range(GROUP):
-        sib_copy(i).start()
-        own_copy(i).start()
-        qsib_copy(i).start()
-        qown_copy(i).start()
-
-    ends = (has_up, has_down)
-    for i in range(GROUP):
+    def send_q(i):
+        for c in range(2):
+            q_copy(i, c).start()
+
+    def send_y(i):
         for d in range(2):
             @pl.when(sides[d][0])
             def _():
                 for c in range(2):
                     y_copy(i, d, c).start()
 
-        if i == 0:
-            for t in range(2):
-                rows = row_bias(chip, chips, t)
-                q_col = iota((TILE, KEYS), 0) % COLS
-                k_col = iota((TILE, KEYS), 1) % COLS
-                for s in range(3):
-                    delta = k_col - q_col + (s - 1) * 2 * COLS
-                    inside = (strip + s - 1 >= 0) & (strip + s - 1 < strips)
-                    ok = rows & (delta >= -HALF) & (delta < HALF)
-                    own_bias[t, s] = jnp.where(ok & inside, 0.0, MASKED)
-                for n in range(2):
-                    at = strip + n - half
-                    far_bias[t, n] = jnp.where(rows & (at >= 0) & (at < strips), 0.0, MASKED)
-
+    def send_here(i):
+        sib_copy(i).start()
+        own_copy(i).start()
+        qsib_copy(i).start()
+        qown_copy(i).start()
+
+    loaded(0)
+    send_z(0)
+    send_y(0)
+    send_q(0)
+    loaded(1)
+    send_z(1)
+    send_here(0)
+    loaded(2)
+    send_z(2)
+    send_q(1)
+    loaded(3)
+    send_z(3)
+    send_q(2)
+    send_q(3)
+    for i in range(1, GROUP):
+        send_here(i)
+
+    ends = (has_up, has_down)
+
+    for i in range(GROUP):
+        if i > 0:
+            send_y(i)
         for n in range(2):
             @pl.when(ends[n])
             def _():

time: 83.9 us -> 82.4 us (0.982)
  Pallas kernels: 82.9 us -> 80.6 us
    pallas_call x1, Pallas kernels: 82.9 us -> 80.6 us  [shards(): pl.pallas_call(functools.partial(kernel, chips, strips), out_shape=pltpu....]
where the time goes in v3:
time: 82.4 us; the launch traced here: 81.3 us
  Pallas kernels  80.6 us (98%)
    pallas_call x1, Pallas kernels, shards(): pl.pallas_call(functools.partial(kernel, chips, strips), out_shape=pltpu....  80.6 us

profile of v3, /device:TPU:1, one launch (start us, length us, event | category | flops | bytes accessed | tf_op | source)
XLA Modules:
  0.0 81.3 jit_solution(14329002103576776937)
XLA Ops:
  0.0 80.6 %shard_map.73 = bf16[128,1024]{1,0:T(8,128)(2,1)S(1)} custom-call(bf16[128,1024]{1,0:T(8,128)(2,1)} %bitcast.8, bf16[128,1024]{1,0:T(8,128)(2,1)} %bitcast.9, bf16[128,1024]{1,0:T(8,128)(2,1)} %bitcast.10, bf16[128,1024]{1,0:T(8,128)(2,1)} %bitcast.11, bf16[128,1024]{1,0:T(8,128)(2,1)} %bitcast.12, f32[3,3,1024]{2,1,0:T(4,128)} %cw_ref.1, f32[1,1024]{1,0:T(1,128)} %bitcast.13), custom_call_target="tpu_custom_call" | custom-call | tf_op jit(solution)/shard_map/pallas_call | solution.py:415
  80.6 0.7 copy.9

commit v4 on v3

--- a/solution.py
+++ b/solution.py
@@ -71,10 +71,10 @@
     def greet(to_ht, to_wt):
         pl.semaphore_signal(barrier, inc=1, device_id={"ht": to_ht, "wt": to_wt}, device_id_type=MESH)
 
+    for c in range(2):
+        greet(2 * chip + c, far)
     greet(2 * chip + other, wt)
     for c in range(2):
-        greet(2 * chip + c, far)
-
         @pl.when(has_up)
         def _():
             greet(2 * (chip - 1) + c, wt)
@@ -202,8 +202,8 @@
                 z_copy(i, c).start()
 
     def send_q(i):
-        for c in range(2):
-            q_copy(i, c).start()
+        q_copy(i, core).start()
+        q_copy(i, other).start()
 
     def send_y(i):
         for d in range(2):

time: 82.4 us -> 82.3 us (level)
  no operation moved by 1% of the time
where the time goes in v4:
time: 82.3 us; the launch traced here: 81.2 us
  Pallas kernels  80.5 us (98%)
    pallas_call x1, Pallas kernels, shards(): pl.pallas_call(functools.partial(kernel, chips, strips), out_shape=pltpu....  80.5 us

profile of v4, /device:TPU:1, one launch (start us, length us, event | category | flops | bytes accessed | tf_op | source)
XLA Modules:
  0.0 81.2 jit_solution(13640537389107336227)
XLA Ops:
  0.0 80.5 %shard_map.73 = bf16[128,1024]{1,0:T(8,128)(2,1)S(1)} custom-call(bf16[128,1024]{1,0:T(8,128)(2,1)} %bitcast.8, bf16[128,1024]{1,0:T(8,128)(2,1)} %bitcast.9, bf16[128,1024]{1,0:T(8,128)(2,1)} %bitcast.10, bf16[128,1024]{1,0:T(8,128)(2,1)} %bitcast.11, bf16[128,1024]{1,0:T(8,128)(2,1)} %bitcast.12, f32[3,3,1024]{2,1,0:T(4,128)} %cw_ref.1, f32[1,1024]{1,0:T(1,128)} %bitcast.13), custom_call_target="tpu_custom_call" | custom-call | tf_op jit(solution)/shard_map/pallas_call | solution.py:415
  80.5 0.7 copy.9
